TPU v7x, 32 devices: a whole 2x2x4 slice. The times are simulated.
32 devices in a mesh: grp: 8 (over z, x), own: 4 (over y, core).
Axes of the slice: x: 2, y: 2, z: 4, core: 2. Of those that a mesh axis runs over, the one named last changes fastest.
Arguments:
- queries: bfloat16 [2048, 768], P(('grp', 'own')), may hold values from -6 to 6
- projection: bfloat16 [768, 768], replicated, may hold values from -0.21875 to 0.21875
- lists: bfloat16 [1024, 256, 768], P(('grp', 'own')), may hold values from -6 to 6
- probes: int32 [2048, 8], P(('grp', 'own')), may hold values from 0 to 1023, as said below
- owner_map: int32 [1024], replicated, may hold values from 0 to 1023, as said below
Outputs:
- scores: float32 [2048, 8, 256], P(('grp', 'own'))
Inputs may be any that keep to these rules, and one draw needn't show every extreme that they name: A permutation: list i is stored in slot owner_map[i], slots k * 32 to (k + 1) * 32 - 1 lying on the k-th device of grp+own. `probes`: a query's 8 list ids are distinct; the 64 queries of one device probe lists stored on any one device at most 32 times in all; all queries together probe any one stored list at most 32 times.
All inputs are finite; a program needn't handle non-finite values.
Results may differ from a plain program's by a relative error of at most 0.0003.
Values may be sent and summed in bfloat16 or wider, within the bound.
A program may use at most 64 MiB of HBM per device.

v0:
```python
import jax
import jax.numpy as jnp
from jax import lax
from jax.sharding import PartitionSpec as P


def rank_within(labels, label_count):
    onehot = (labels[:, None] == jnp.arange(label_count, dtype=jnp.int32)[None, :]).astype(
        jnp.int32
    )
    before = jnp.cumsum(onehot, axis=0) - onehot
    return jnp.sum(before * onehot, axis=1)


def body(queries, projection, lists, probes, owner_map):
    query_count = queries.shape[0]
    width = queries.shape[1]
    probe_count = probes.shape[1]
    lists_here = lists.shape[0]
    list_size = lists.shape[1]
    group_count = lax.axis_size("grp")
    owner_count = lax.axis_size("own")
    device_count = group_count * owner_count
    capacity = 2 * query_count * probe_count // device_count
    list_capacity = device_count * capacity // lists_here
    projected = jnp.dot(queries, projection, preferred_element_type=jnp.float32).astype(
        jnp.bfloat16
    )
    stored = jnp.take(owner_map, probes.reshape(-1))
    target = stored // lists_here
    local = stored % lists_here
    position = target * capacity + rank_within(target, device_count)
    query_of = jnp.arange(query_count * probe_count, dtype=jnp.int32) // probe_count
    send_rows = (
        jnp.zeros((device_count * capacity, width), jnp.bfloat16)
        .at[position]
        .set(projected[query_of])
    )
    send_lists = (
        jnp.full((device_count * capacity,), -1.0, jnp.bfloat16)
        .at[position]
        .set(local.astype(jnp.bfloat16))
    )
    got_rows, got_lists = (
        lax.all_to_all(
            send_rows.reshape(device_count, capacity, width),
            ("grp", "own"),
            split_axis=0,
            concat_axis=0,
            tiled=True,
        ),
        lax.all_to_all(
            send_lists.reshape(device_count, capacity),
            ("grp", "own"),
            split_axis=0,
            concat_axis=0,
            tiled=True,
        ),
    )
    got_rows = got_rows.reshape(device_count * capacity, width)
    list_index = got_lists.reshape(-1).astype(jnp.int32)
    valid = list_index >= 0
    safe_index = jnp.where(valid, list_index, lists_here)
    spot = jnp.where(
        valid,
        safe_index * list_capacity + rank_within(safe_index, lists_here),
        lists_here * list_capacity,
    )
    grouped = (
        jnp.zeros((lists_here * list_capacity, width), jnp.bfloat16)
        .at[spot]
        .set(got_rows, mode="drop")
    )
    grouped = grouped.reshape(lists_here, list_capacity, width)
    dots = jnp.einsum("lcd,lvd->lcv", grouped, lists, preferred_element_type=jnp.float32)
    vec_norm = jnp.einsum("lvd,lvd->lv", lists, lists, preferred_element_type=jnp.float32)
    row_norm = jnp.einsum("lcd,lcd->lc", grouped, grouped, preferred_element_type=jnp.float32)
    distance = (row_norm[:, :, None] + vec_norm[:, None, :] - 2.0 * dots) / width
    flat_dist = distance.reshape(lists_here * list_capacity, list_size)
    answers = flat_dist[jnp.minimum(spot, lists_here * list_capacity - 1)]
    answers = jnp.where(valid[:, None], answers, 0.0)
    returned = lax.all_to_all(
        answers.reshape(device_count, capacity, list_size),
        ("grp", "own"),
        split_axis=0,
        concat_axis=0,
        tiled=True,
    )
    returned = returned.reshape(device_count * capacity, list_size)
    return returned[position].reshape(query_count, probe_count, list_size)


def solution(mesh):
    placed = (
        P(("grp", "own"), None),
        P(),
        P(("grp", "own"), None, None),
        P(("grp", "own"), None),
        P(),
    )
    return jax.shard_map(
        body, mesh=mesh, in_specs=placed, out_specs=P(("grp", "own"), None, None), check_vma=False
    )
```

profile of v0, /device:TPU:0, one launch (start us, length us, event | category | flops | bytes accessed | tf_op | source)
XLA Modules:
  0.0 121.9 jit_solution(1066642360295279037)
XLA Ops:
  0.0 0.0 copy-start
  0.0 0.0 copy-start.1
  0.0 0.0 copy-start.4
  0.0 0.9 copy.18
  0.9 0.1 reshape.329
  1.0 0.1 reshape.331
  1.1 0.1 reshape.330
  1.2 0.0 copy-done.1
  1.2 2.3 %gather_fusion = s32[512]{0:T(512)S(1)} fusion(s32[1024]{0:T(1024)S(1)} %copy-done.1, s32[1024]{0:T(1024)S(1)} %pad_clamp_fusion.2), kind=kCustom, calls=%fused_computation | custom fusion | bytes 6144 | tf_op jit(solution)/shard_map/jit(_take)/gather | solution.py:29
  3.5 1.2 reduce-window.14
  4.7 0.2 slice_reduce_fusion
  5.0 0.1 fusion.15
  5.1 3.8 %scatter_custom_fusion = bf16[1024]{0:T(1024)(128)(2,1)S(1)} fusion(s32[512]{0:T(512)S(1)} %bitcast.81, bf16[512]{0:T(512)(128)(2,1)S(1)} %get-tuple-element.7, bf16[]{:T(256)} %constant.69.clone.1), kind=kCustom, calls=%fused_computation.84 | custom fusion | bytes 2050 | tf_op jit(solution)/shard_map/scatter | solution.py:42
  8.9 0.7 all_to_all.16
  9.6 7.3 %all-to-all-start = ((bf16[32,1,32]{2,1,0:T(2,128)(2,1)}), bf16[32,1,32]{2,1,0:T(2,128)(2,1)S(1)}, u32[]{:S(2)}, u32[]{:S(2)}) async-start(bf16[32,1,32]{2,1,0:T(2,128)(2,1)} %all_to_all.16), calls=%async_computation | async-start | bytes 32768 | tf_op jit(solution)/shard_map/all_to_all | solution.py:52
  16.9 0.0 copy-done
  16.9 0.0 copy-done.4
  16.9 0.3 convolution_convert_fusion
  17.3 6.7 %scatter_custom_fusion.1 = bf16[1024,768]{1,0:T(8,128)(2,1)} fusion(s32[512]{0:T(512)S(1)} %bitcast.82, bf16[64,768]{1,0:T(8,128)(2,1)S(1)} %convolution_convert_fusion, s32[1024]{0:T(1024)S(1)} %pad_clamp_fusion.1, bf16[]{:T(256)} %constant.79.clone.1), kind=kCustom, calls=%fused_computation.15 | custom fusion | bytes 1572866 | tf_op jit(solution)/shard_map/scatter | solution.py:37
  24.0 0.0 all-to-all-done
  24.0 6.0 %all-to-all-start.1 = ((bf16[32,32,768]{2,1,0:T(8,128)(2,1)}), bf16[32,32,768]{2,1,0:T(8,128)(2,1)S(1)}, u32[]{:S(2)}, u32[]{:S(2)}) async-start(bf16[32,32,768]{2,1,0:T(8,128)(2,1)} %bitcast.12), calls=%async_computation.1 | async-start | bytes 3145728 | tf_op jit(solution)/shard_map/all_to_all | solution.py:45
  30.0 7.1 %fusion = f32[32,256]{1,0:T(8,128)S(1)} fusion(bf16[32,256,768]{2,1,0:T(8,128)(2,1)} %param.7), kind=kLoop, calls=%fused_computation.8 | loop fusion | flops 18866176 | bytes 12615680 | tf_op jit(solution)/shard_map/lvd,lvd->lv/dot_general | solution.py:76
  37.2 0.1 reshape.342
  37.2 0.1 reshape.341
  37.3 0.1 reshape.340
  37.4 9.0 %reduce-window.16 = s32[32,8,128]{2,1,0:T(8,128)S(1)} reduce-window(s32[32,8,128]{2,1,0:T(8,128)S(1)} %fusion.12, s32[]{:T(128)} %constant.70.clone.1), window={size=1x1x128 pad=0_0x0_0x127_0}, to_apply=%region_4.5 | reduce-window | flops 4161536 | bytes 262148 | tf_op jit(solution)/shard_map/reduce-window.2
  46.4 0.1 slice.25
  46.5 0.1 copy.24
  46.7 0.1 copy.25
  46.8 0.1 broadcast_add_fusion
  47.0 20.4 %all-to-all-done.1 = bf16[32,32,768]{2,1,0:T(8,128)(2,1)S(1)} async-done(((bf16[32,32,768]{2,1,0:T(8,128)(2,1)}), bf16[32,32,768]{2,1,0:T(8,128)(2,1)S(1)}, u32[]{:S(2)}, u32[]{:S(2)}) %all-to-all-start.1) | async-done | bytes 1572896 | tf_op jit(solution)/shard_map/all_to_all | solution.py:45
  67.4 0.0 copy-start.3
  67.4 1.2 copy-done.3
  68.5 6.2 %scatter_custom_fusion.2 = bf16[1024,768]{1,0:T(8,128)(2,1)S(1)} fusion(s32[1024]{0:T(1024)S(1)} %bitcast.85, bf16[1024,768]{1,0:T(8,128)(2,1)} %bitcast.73, bf16[]{:T(256)} %constant.79.clone.1), kind=kCustom, calls=%fused_computation.17 | custom fusion | bytes 1573376 | tf_op jit(solution)/shard_map/scatter | solution.py:72
  74.7 0.0 copy-start.2
  74.7 1.1 copy-done.2
  75.9 0.4 fusion.1
  76.3 8.8 %fusion.3 = f32[32,32,256]{2,1,0:T(8,128)S(1)} fusion(bf16[32,32,768]{2,1,0:T(8,128)(2,1)} %bitcast.71, bf16[32,256,768]{2,1,0:T(8,128)(2,1)} %param.7, f32[32,256]{1,0:T(8,128)S(1)} %fusion, f32[32,32]{1,0:T(8,128)S(1)} %fusion.1), kind=kOutput, calls=%fused_computation.13 | convolution fusion | flops 403701760 | bytes 15241216 | tf_op jit(solution)/shard_map/lcd,lvd->lcv/dot_general | solution.py:75
  85.1 3.5 %gather_fusion.1 = f32[1024,256]{1,0:T(8,128)S(1)} fusion(f32[1024,256]{1,0:T(8,128)S(1)} %bitcast.68, s32[1024]{0:T(1024)S(1)} %broadcast_clamp_fusion), kind=kCustom, calls=%fused_computation.2 | custom fusion | bytes 2101248 | tf_op jit(solution)/shard_map/gather | solution.py:80
  88.6 1.2 broadcast_select_fusion
  89.8 3.7 %all-to-all-start.2 = ((f32[32,32,256]{2,1,0:T(8,128)}), f32[32,32,256]{2,1,0:T(8,128)S(1)}, u32[]{:S(2)}, u32[]{:S(2)}) async-start(f32[32,32,256]{2,1,0:T(8,128)} %broadcast_select_fusion), calls=%async_computation.2 | async-start | bytes 2097152 | tf_op jit(solution)/shard_map/all_to_all | solution.py:82
  93.4 26.2 %all-to-all-done.2 = f32[32,32,256]{2,1,0:T(8,128)S(1)} async-done(((f32[32,32,256]{2,1,0:T(8,128)}), f32[32,32,256]{2,1,0:T(8,128)S(1)}, u32[]{:S(2)}, u32[]{:S(2)}) %all-to-all-start.2) | async-done | bytes 1048608 | tf_op jit(solution)/shard_map/all_to_all | solution.py:82
  119.7 2.2 %gather_fusion.2 = f32[512,256]{1,0:T(8,128)} fusion(f32[1024,256]{1,0:T(8,128)S(1)} %bitcast.69, s32[1024]{0:T(1024)S(1)} %pad_clamp_fusion), kind=kCustom, calls=%fused_computation.3 | custom fusion | bytes 1050624 | tf_op jit(solution)/shard_map/gather | solution.py:90
  (22 shorter events, 0.3 us)
Async XLA Ops:
  0.0 16.9 %copy-start = (bf16[768,768]{1,0:T(8,128)(2,1)S(1)}, bf16[768,768]{1,0:T(8,128)(2,1)}, u32[]{:S(2)}) copy-start(bf16[768,768]{1,0:T(8,128)(2,1)} %param.6) | copy-start | bytes 3538948
  0.0 1.2 copy-start.1
  0.0 16.9 %copy-start.4 = (bf16[64,768]{1,0:T(8,128)(2,1)S(1)}, bf16[64,768]{1,0:T(8,128)(2,1)}, u32[]{:S(2)}) copy-start(bf16[64,768]{1,0:T(8,128)(2,1)} %param.5) | copy-start | bytes 294916
  9.6 14.4 %all-to-all-start = ((bf16[32,1,32]{2,1,0:T(2,128)(2,1)}), bf16[32,1,32]{2,1,0:T(2,128)(2,1)S(1)}, u32[]{:S(2)}, u32[]{:S(2)}) async-start(bf16[32,1,32]{2,1,0:T(2,128)(2,1)} %all_to_all.16), calls=%async_computation | async-start | bytes 32768 | tf_op jit(solution)/shard_map/all_to_all | solution.py:52
  24.0 43.4 %all-to-all-start.1 = ((bf16[32,32,768]{2,1,0:T(8,128)(2,1)}), bf16[32,32,768]{2,1,0:T(8,128)(2,1)S(1)}, u32[]{:S(2)}, u32[]{:S(2)}) async-start(bf16[32,32,768]{2,1,0:T(8,128)(2,1)} %bitcast.12), calls=%async_computation.1 | async-start | bytes 3145728 | tf_op jit(solution)/shard_map/all_to_all | solution.py:45
  67.4 1.2 copy-start.3
  74.7 1.2 copy-start.2
  89.8 29.9 %all-to-all-start.2 = ((f32[32,32,256]{2,1,0:T(8,128)}), f32[32,32,256]{2,1,0:T(8,128)S(1)}, u32[]{:S(2)}, u32[]{:S(2)}) async-start(f32[32,32,256]{2,1,0:T(8,128)} %broadcast_select_fusion), calls=%async_computation.2 | async-start | bytes 2097152 | tf_op jit(solution)/shard_map/all_to_all | solution.py:82
where the time goes:
time: 122 us
  waiting for transfers between devices  46.6 us (38%)
  local copies, waits for them, and re-layouts  29.6 us (24%)
  other arithmetic  19.3 us (16%)
  starting transfers between devices  17 us (14%)
  matrix products  9.15 us (8%)
    all_to_all x1, waiting for transfers between devices, body(): lax.all_to_all(answers.reshape(device_count, capacity, list_size), ('grp'...  26.2 us
    all_to_all x1, waiting for transfers between devices, body(): lax.all_to_all(send_rows.reshape(device_count, capacity, width), ('grp',...  20.4 us
    another operation x5, other arithmetic  10.3 us
    dot_general x1, matrix products, body(): jnp.einsum('lcd,lvd->lcv', grouped, lists, preferred_element_type=jnp.flo...  8.82 us
    all_to_all x1, starting transfers between devices, body(): lax.all_to_all(send_lists.reshape(device_count, capacity), ('grp', 'own')...  7.3 us
    dot_general x1, other arithmetic, body(): jnp.einsum('lvd,lvd->lv', lists, lists, preferred_element_type=jnp.float32)  7.11 us
    scatter x1, local copies, waits for them, and re-layouts, body(): send_rows = jnp.zeros((device_count * capacity, width), jnp.bfloat16).at[...  6.74 us
    scatter x1, local copies, waits for them, and re-layouts, body(): grouped = jnp.zeros((lists_here * list_capacity, width), jnp.bfloat16).at...  6.21 us
  transfers between devices with their start and end apart: 3, of which 2 were waited for; matrix products, arithmetic and copies ran while one was open for 20% of the time, Pallas kernels for 0%

commit v1 on v0

v1 whole, which is shorter than its diff:
```python
import jax
import jax.numpy as jnp
from jax import lax
from jax.sharding import PartitionSpec as P

AXES = ("grp", "own")


def body(queries, projection, lists, probes, owner_map):
    query_count, width = queries.shape
    probe_count = probes.shape[1]
    lists_here, list_size = lists.shape[0], lists.shape[1]
    device_count = lax.axis_size("grp") * lax.axis_size("own")
    pairs = query_count * probe_count
    capacity = 2 * pairs // device_count
    list_capacity = device_count * capacity // lists_here
    slots = device_count * capacity
    me = lax.axis_index(AXES)

    projected = jnp.dot(queries, projection, preferred_element_type=jnp.float32).astype(
        jnp.bfloat16
    )
    stored = jnp.take(owner_map, probes.reshape(-1))
    target = stored // lists_here
    local = stored % lists_here
    to_target = (target[:, None] == jnp.arange(device_count, dtype=jnp.int32)[None, :]).astype(
        jnp.bfloat16
    )
    step = jnp.arange(pairs, dtype=jnp.int32)
    earlier = (step[None, :] < step[:, None]).astype(jnp.bfloat16)
    before = jnp.dot(earlier, to_target, preferred_element_type=jnp.float32)
    rank = jnp.sum(before * to_target.astype(jnp.float32), axis=1).astype(jnp.int32)
    position = target * capacity + rank

    at_rank = (rank[:, None] == jnp.arange(capacity, dtype=jnp.int32)[None, :]).astype(jnp.bfloat16)
    query_of = step // probe_count
    what = jnp.stack([jnp.ones_like(step), query_of, local], axis=0).astype(jnp.bfloat16)
    weighted = to_target.T[None] * what[:, None, :]
    table = jnp.dot(
        weighted.reshape(3 * device_count, pairs), at_rank, preferred_element_type=jnp.float32
    ).reshape(3, device_count, capacity)
    table = jnp.where(table[:1] > 0.5, table[1:], -1.0).astype(jnp.bfloat16)
    extra = -(-(2 * slots) // width)
    extra = -(-extra // 16) * 16
    table = jnp.pad(table.reshape(-1), (0, extra * width - 2 * slots)).reshape(extra, width)

    everyone = lax.all_gather(jnp.concatenate([projected, table], axis=0), AXES, tiled=False)
    rows = everyone[:, :query_count].reshape(device_count * query_count, width)
    tables = everyone[:, query_count:].reshape(device_count, -1)[:, : 2 * slots]
    tables = tables.reshape(device_count, 2, device_count, capacity)
    mine = lax.dynamic_index_in_dim(tables, me, axis=2, keepdims=False).astype(jnp.int32)
    asked_query = mine[:, 0].reshape(-1)
    asked_list = mine[:, 1].reshape(-1)
    row_of = (
        asked_query + query_count * (jnp.arange(slots, dtype=jnp.int32) // capacity)
    )

    in_list = (asked_list[:, None] == jnp.arange(lists_here, dtype=jnp.int32)[None, :]).astype(
        jnp.bfloat16
    )
    place = jnp.arange(slots, dtype=jnp.int32)
    earlier = (place[None, :] < place[:, None]).astype(jnp.bfloat16)
    before = jnp.dot(earlier, in_list, preferred_element_type=jnp.float32)
    order = jnp.sum(before * in_list.astype(jnp.float32), axis=1).astype(jnp.int32)
    valid = asked_list >= 0
    spot = jnp.where(valid, asked_list * list_capacity + order, -1)
    hit = spot[:, None] == jnp.arange(lists_here * list_capacity, dtype=jnp.int32)[None, :]
    grouped_row = jnp.sum(jnp.where(hit, row_of[:, None], 0), axis=0)
    grouped = rows[grouped_row].reshape(lists_here, list_capacity, width)

    dots = jnp.einsum("lcd,lvd->lcv", grouped, lists, preferred_element_type=jnp.float32)
    vec_norm = jnp.einsum("lvd,lvd->lv", lists, lists, preferred_element_type=jnp.float32)
    row_norm = jnp.einsum("lcd,lcd->lc", grouped, grouped, preferred_element_type=jnp.float32)
    distance = (row_norm[:, :, None] + vec_norm[:, None, :] - 2.0 * dots) / width
    flat_dist = distance.reshape(lists_here * list_capacity, list_size)
    answers = flat_dist[jnp.maximum(spot, 0)]
    returned = lax.all_to_all(
        answers.reshape(device_count, capacity, list_size),
        AXES,
        split_axis=0,
        concat_axis=0,
        tiled=True,
    )
    returned = returned.reshape(slots, list_size)
    return returned[position].reshape(query_count, probe_count, list_size)


def solution(mesh):
    placed = (
        P(AXES, None),
        P(),
        P(AXES, None, None),
        P(AXES, None),
        P(),
    )
    return jax.shard_map(
        body, mesh=mesh, in_specs=placed, out_specs=P(AXES, None, None), check_vma=False
    )
```

time: 122 us -> 145 us (1.19)
  waiting for transfers between devices: 46.6 us -> 83.2 us
  starting transfers between devices: 17 us -> 3.28 us
  between operations: 0.27 us -> 13.7 us
  other arithmetic: 19.3 us -> 9.31 us
  local copies, waits for them, and re-layouts: 29.6 us -> 25.3 us
    all_gather x0 -> x1, waiting for transfers between devices: none -> 57 us  [body(): lax.all_gather(jnp.concatenate([projected, table], axis=0), AXES, tiled=F...]
    all_to_all x3 -> x1, waiting for transfers between devices: 46.6 us -> 26.2 us  [body(): lax.all_to_all(answers.reshape(device_count, capacity, list_size), AXES,...]
    scatter x3 -> x0, local copies, waits for them, and re-layouts: 16.7 us -> none  [the longest x1 6.74 us: body(): send_rows = jnp.zeros((device_count * capacity, width), jnp.bfloat16).at[...]
    all_to_all x3 -> x1, starting transfers between devices: 17 us -> 3.28 us  [body(): lax.all_to_all(answers.reshape(device_count, capacity, list_size), AXES,...]
    another operation x5 -> x2, other arithmetic: 10.3 us -> 0.1 us  [the longest x1 0.08 us: body(): jnp.stack([jnp.ones_like(step), query_of, local], axis=0)]
    gather x1 -> x2, local copies, waits for them, and re-layouts: 3.47 us -> 11.4 us  [the longest x1 6.77 us: body(): grouped = rows[grouped_row].reshape(lists_here, list_capacity, width)]
    slice x1 -> x6, local copies, waits for them, and re-layouts: 0.22 us -> 5.39 us  [the longest x1 3.91 us: body(): rows = everyone[:, :query_count].reshape(device_count * query_count, width)]
    unnamed x11 -> x8, local copies, waits for them, and re-layouts: 3.19 us -> 1.7 us
  transfers between devices with their start and end apart: 3 -> 2, of which waited for: 2 -> 2; matrix products, arithmetic and copies ran while one was open for 20% -> 5% of each run, Pallas kernels for 0% -> 0%
where the time goes in v1:
time: 145 us
  waiting for transfers between devices  83.2 us (57%)
  local copies, waits for them, and re-layouts  25.3 us (17%)
  between operations  13.7 us (9%)
  matrix products  10.2 us (7%)
  other arithmetic  9.31 us (6%)
  starting transfers between devices  3.28 us (2%)
    all_gather x1, waiting for transfers between devices, body(): lax.all_gather(jnp.concatenate([projected, table], axis=0), AXES, tiled=F...  57 us
    all_to_all x1, waiting for transfers between devices, body(): lax.all_to_all(answers.reshape(device_count, capacity, list_size), AXES,...  26.2 us
    dot_general x1, matrix products, body(): jnp.einsum('lcd,lvd->lcv', grouped, lists, preferred_element_type=jnp.flo...  8.82 us
    dot_general x1, other arithmetic, body(): jnp.einsum('lvd,lvd->lv', lists, lists, preferred_element_type=jnp.float32)  7.11 us
    gather x1, local copies, waits for them, and re-layouts, body(): grouped = rows[grouped_row].reshape(lists_here, list_capacity, width)  6.77 us
    gather x1, local copies, waits for them, and re-layouts, body(): answers = flat_dist[jnp.maximum(spot, 0)]  4.67 us
    slice x1, local copies, waits for them, and re-layouts, body(): rows = everyone[:, :query_count].reshape(device_count * query_count, width)  3.91 us
    gather x1, local copies, waits for them, and re-layouts, body(): stored = jnp.take(owner_map, probes.reshape(-1))  3.37 us
  transfers between devices with their start and end apart: 2, of which 2 were waited for; matrix products, arithmetic and copies ran while one was open for 5% of the time, Pallas kernels for 0%

profile of v1, /device:TPU:0, one launch (start us, length us, event | category | flops | bytes accessed | tf_op | source)
XLA Modules:
  0.0 145.1 jit_solution(16968780220020066380)
XLA Ops:
  6.5 0.0 copy-start
  6.5 0.0 copy-start.2
  6.5 0.0 all-gather.3.cloned.1.call-start
  6.5 0.9 copy.17
  7.4 0.1 reshape.426
  7.5 0.1 reshape.427
  7.6 0.1 reshape.425
  7.7 3.4 %gather_fusion = s32[512]{0:T(512)S(1)} fusion(s32[1024]{0:T(1024)} %param.9, s32[1024]{0:T(1024)S(1)} %pad_clamp_fusion.1), kind=kCustom, calls=%fused_computation | custom fusion | bytes 6144 | tf_op jit(solution)/shard_map/jit(_take)/gather | solution.py:23
  11.1 0.3 fusion.7
  11.4 0.1 pad_maximum_fusion.1
  11.5 0.3 fusion.8
  11.8 0.1 slice.42
  12.0 0.1 copy.21
  12.0 0.1 slice.27
  12.1 0.1 copy.20
  12.2 0.1 broadcast_in_dim.64
  12.4 0.0 copy-done
  12.4 0.0 copy-done.2
  12.4 0.3 convolution_convert_fusion
  12.8 0.7 pad_maximum_fusion
  13.4 0.0 all-gather.3.cloned.1.call-update
  13.5 7.1 %fusion = f32[32,256]{1,0:T(8,128)S(1)} fusion(bf16[32,256,768]{2,1,0:T(8,128)(2,1)} %param.7), kind=kLoop, calls=%fused_computation.5 | loop fusion | flops 18866176 | bytes 12615680 | tf_op jit(solution)/shard_map/lvd,lvd->lv/dot_general | solution.py:72
  20.6 57.0 %all-gather.3.cloned.1.call-done = bf16[2560,768]{1,0:T(8,128)(2,1)} async-done(((bf16[80,768]{1,0:T(8,128)(2,1)}), bf16[2560,768]{1,0:T(8,128)(2,1)}) %all-gather.3.cloned.1.call-update) | async-done | bytes 3932176 | tf_op jit(solution)/shard_map/all_gather | solution.py:47
  77.6 1.2 slice.44
  78.8 3.9 %slice.43 = bf16[32,64,768]{2,1,0:T(8,128)(2,1)} slice(bf16[32,80,768]{2,1,0:T(8,128)(2,1)} %bitcast.32), slice={[0:32], [0:64], [0:768]} | slice | bytes 6291456 | tf_op jit(solution)/shard_map/slice | solution.py:48
  82.7 0.2 copy.30
  83.0 0.4 reshape.431
  83.3 0.1 dynamic-slice_convert_fusion
  83.4 0.1 multiply_reduce_fusion
  83.5 0.1 reshape_squeeze.6
  83.6 0.5 fusion.6
  84.2 0.1 compare_reduce_fusion
  84.3 0.1 reshape_squeeze.7
  84.3 0.6 select_reduce_fusion
  85.0 6.8 %gather_fusion.1 = bf16[1024,768]{1,0:T(8,128)(2,1)S(1)} fusion(bf16[2048,768]{1,0:T(8,128)(2,1)} %bitcast.27, s32[1024]{0:T(1024)S(1)} %broadcast_clamp_fusion), kind=kCustom, calls=%fused_computation.1 | custom fusion | bytes 3149824 | tf_op jit(solution)/shard_map/gather | solution.py:69
  91.8 0.0 copy-start.1
  91.8 0.4 fusion.2
  92.2 0.1 mul.91
  92.3 0.1 ge.54
  92.4 0.6 copy-done.1
  93.0 8.8 %fusion.4 = f32[32,32,256]{2,1,0:T(8,128)S(1)} fusion(bf16[32,32,768]{2,1,0:T(8,128)(2,1)} %bitcast.30, bf16[32,256,768]{2,1,0:T(8,128)(2,1)} %param.7, f32[32,256]{1,0:T(8,128)S(1)} %fusion, f32[32,32]{1,0:T(8,128)S(1)} %fusion.2), kind=kOutput, calls=%fused_computation.14 | convolution fusion | flops 403701760 | bytes 15241216 | tf_op jit(solution)/shard_map/lcd,lvd->lcv/dot_general | solution.py:71
  101.8 4.7 %gather_fusion.2 = f32[1024,256]{1,0:T(8,128)} fusion(f32[1024,256]{1,0:T(8,128)S(1)} %bitcast.26, s32[1024]{0:T(1024)S(1)} %broadcast_clamp_fusion.1), kind=kCustom, calls=%fused_computation.2 | custom fusion | bytes 2101248 | tf_op jit(solution)/shard_map/gather | solution.py:76
  106.5 3.3 %all-to-all-start = ((f32[32,32,256]{2,1,0:T(8,128)}), f32[32,32,256]{2,1,0:T(8,128)S(1)}, u32[]{:S(2)}, u32[]{:S(2)}) async-start(f32[32,32,256]{2,1,0:T(8,128)} %bitcast.12), calls=%async_computation | async-start | bytes 2097152 | tf_op jit(solution)/shard_map/all_to_all | solution.py:77
  109.8 26.2 %all-to-all-done = f32[32,32,256]{2,1,0:T(8,128)S(1)} async-done(((f32[32,32,256]{2,1,0:T(8,128)}), f32[32,32,256]{2,1,0:T(8,128)S(1)}, u32[]{:S(2)}, u32[]{:S(2)}) %all-to-all-start) | async-done | bytes 1048608 | tf_op jit(solution)/shard_map/all_to_all | solution.py:77
  136.0 2.2 %gather_fusion.3 = f32[512,256]{1,0:T(8,128)} fusion(f32[1024,256]{1,0:T(8,128)S(1)} %bitcast.28, s32[1024]{0:T(1024)S(1)} %pad_clamp_fusion), kind=kCustom, calls=%fused_computation.3 | custom fusion | bytes 1050624 | tf_op jit(solution)/shard_map/gather | solution.py:85
  (23 shorter events, 0.3 us)
Async XLA Ops:
  6.5 5.9 %copy-start = (bf16[768,768]{1,0:T(8,128)(2,1)S(1)}, bf16[768,768]{1,0:T(8,128)(2,1)}, u32[]{:S(2)}) copy-start(bf16[768,768]{1,0:T(8,128)(2,1)} %param.6) | copy-start | bytes 3538948
  6.5 5.9 %copy-start.2 = (bf16[64,768]{1,0:T(8,128)(2,1)S(1)}, bf16[64,768]{1,0:T(8,128)(2,1)}, u32[]{:S(2)}) copy-start(bf16[64,768]{1,0:T(8,128)(2,1)} %param.5) | copy-start | bytes 294916
  6.5 71.1 %all-gather.3.cloned.1.call-start = ((), (), s32[]{:S(2)}) async-start(), calls=%async_computation.1 | async-start | bytes 4055040 | tf_op jit(solution)/shard_map/all_gather | solution.py:47
  91.8 1.2 copy-start.1
  106.5 29.5 %all-to-all-start = ((f32[32,32,256]{2,1,0:T(8,128)}), f32[32,32,256]{2,1,0:T(8,128)S(1)}, u32[]{:S(2)}, u32[]{:S(2)}) async-start(f32[32,32,256]{2,1,0:T(8,128)} %bitcast.12), calls=%async_computation | async-start | bytes 2097152 | tf_op jit(solution)/shard_map/all_to_all | solution.py:77
Sparse Core Ops, SparseCore 0:
  13.6 63.9 all-gather.2

commit v2 on v1

--- a/solution.py
+++ b/solution.py
@@ -1,9 +1,103 @@
 import jax
 import jax.numpy as jnp
 from jax import lax
+from jax.experimental import pallas as pl
+from jax.experimental.pallas import tpu as pltpu
 from jax.sharding import PartitionSpec as P
 
 AXES = ("grp", "own")
+LANES = 128
+
+
+def gather_kernel(mine_ref, all_ref, send_sem, recv_sem):
+    grp, own = lax.axis_index("grp"), lax.axis_index("own")
+    z, x, y, c = grp // 2, grp % 2, own // 2, own % 2
+
+    def device(zz, xx, yy, cc):
+        return (zz * 2 + xx, yy * 2 + cc)
+
+    def number(zz, xx, yy, cc):
+        return (zz * 2 + xx) * 4 + yy * 2 + cc
+
+    zs = [z] + [lax.rem(z + k, 4) for k in (1, 2, 3)]
+    over_z = [device(zz, x, y, c) for zz in zs[1:]]
+    over_x, over_y = device(z, 1 - x, y, c), device(z, x, 1 - y, c)
+    sibling = device(z, x, y, 1 - c)
+    barrier = pltpu.get_barrier_semaphore()
+    for peer in over_z + [over_x, over_y, sibling]:
+        pl.semaphore_signal(barrier, inc=1, device_id=peer, device_id_type=pl.DeviceIdType.MESH)
+    pl.semaphore_wait(barrier, 6)
+
+    sent = []
+
+    def describe(src, block, peer, slot):
+        return pltpu.make_async_remote_copy(
+            src_ref=src,
+            dst_ref=all_ref.at[block],
+            send_sem=send_sem.at[slot],
+            recv_sem=recv_sem.at[block],
+            device_id=peer,
+            device_id_type=pl.DeviceIdType.MESH,
+        )
+
+    def send(src, block, peer):
+        copy = describe(src, block, peer, len(sent))
+        copy.start()
+        sent.append(copy)
+
+    def arrived(block):
+        describe(all_ref.at[block], block, sibling, 0).wait_recv()
+        return all_ref.at[block]
+
+    me = number(z, x, y, c)
+    for peer in over_z + [over_x, over_y, sibling]:
+        send(mine_ref, me, peer)
+    all_ref[me] = mine_ref[...]
+    for k in (0, 1, 3, 2):
+        if k:
+            block = number(zs[k], x, y, c)
+            ref = arrived(block)
+            for peer in (over_x, over_y, sibling):
+                send(ref, block, peer)
+        block = number(zs[k], 1 - x, y, c)
+        ref = arrived(block)
+        if k % 2 == 1:
+            send(ref, block, over_y)
+        send(ref, block, sibling)
+        block = number(zs[k], x, 1 - y, c)
+        ref = arrived(block)
+        if k % 2 == 0:
+            send(ref, block, over_x)
+        send(ref, block, sibling)
+    for k in (0, 1, 3, 2):
+        block = number(zs[k], 1 - x, 1 - y, c)
+        send(arrived(block), block, sibling)
+    for k in (0, 1, 3, 2):
+        for xx in (x, 1 - x):
+            for yy in (y, 1 - y):
+                arrived(number(zs[k], xx, yy, 1 - c))
+    for copy in sent:
+        copy.wait_send()
+
+
+def gather_all(block):
+    group_count, owner_count = lax.axis_size("grp"), lax.axis_size("own")
+    if (group_count, owner_count) != (8, 4):
+        return lax.all_gather(block, AXES, tiled=False)
+    device_count = group_count * owner_count
+    return pl.pallas_call(
+        gather_kernel,
+        out_shape=jax.ShapeDtypeStruct((device_count,) + block.shape, block.dtype),
+        in_specs=[pl.BlockSpec(memory_space=pltpu.VMEM)],
+        out_specs=pl.BlockSpec(memory_space=pltpu.VMEM),
+        scratch_shapes=[
+            pltpu.SemaphoreType.DMA((device_count,)),
+            pltpu.SemaphoreType.DMA((device_count,)),
+        ],
+        compiler_params=pltpu.CompilerParams(
+            collective_id=0, has_side_effects=True, vmem_limit_bytes=16 * 2**20
+        ),
+    )(block)
 
 
 def body(queries, projection, lists, probes, owner_map):
@@ -40,13 +134,18 @@
         weighted.reshape(3 * device_count, pairs), at_rank, preferred_element_type=jnp.float32
     ).reshape(3, device_count, capacity)
     table = jnp.where(table[:1] > 0.5, table[1:], -1.0).astype(jnp.bfloat16)
-    extra = -(-(2 * slots) // width)
-    extra = -(-extra // 16) * 16
-    table = jnp.pad(table.reshape(-1), (0, extra * width - 2 * slots)).reshape(extra, width)
+    columns = width // LANES
+    extra = -(-(2 * slots) // (16 * LANES)) * 16
+    table = jnp.pad(table.reshape(-1), (0, extra * LANES - 2 * slots)).reshape(extra, LANES)
+    stacked = projected.reshape(query_count, columns, LANES).transpose(1, 0, 2)
+    stacked = stacked.reshape(columns * query_count, LANES)
 
-    everyone = lax.all_gather(jnp.concatenate([projected, table], axis=0), AXES, tiled=False)
-    rows = everyone[:, :query_count].reshape(device_count * query_count, width)
-    tables = everyone[:, query_count:].reshape(device_count, -1)[:, : 2 * slots]
+    everyone = gather_all(jnp.concatenate([stacked, table], axis=0))
+    rows = everyone[:, : columns * query_count].reshape(
+        device_count, columns, query_count, LANES
+    )
+    rows = rows.transpose(0, 2, 1, 3).reshape(device_count * query_count, width)
+    tables = everyone[:, columns * query_count :].reshape(device_count, -1)[:, : 2 * slots]
     tables = tables.reshape(device_count, 2, device_count, capacity)
     mine = lax.dynamic_index_in_dim(tables, me, axis=2, keepdims=False).astype(jnp.int32)
     asked_query = mine[:, 0].reshape(-1)

time: 145 us -> 114 us (0.79)
  waiting for transfers between devices: 83.2 us -> 26.2 us
  Pallas kernels: 0 us -> 32.3 us
  between operations: 13.7 us -> 0.29 us
  local copies, waits for them, and re-layouts: 25.3 us -> 30 us
  starting transfers between devices: 3.28 us -> 5.53 us
    all_gather x1 -> x0, waiting for transfers between devices: 57 us -> none  [body(): lax.all_gather(jnp.concatenate([projected, table], axis=0), AXES, tiled=F...]
    pallas_call x0 -> x1, Pallas kernels: none -> 32.3 us  [gather_all(): pl.pallas_call(gather_kernel, out_shape=jax.ShapeDtypeStruct((device_coun...]
    reshape x2, local copies, waits for them, and re-layouts: 0.41 us -> 4.94 us  [the longest x1 4.81 us: body(): everyone[:, :columns * query_count]]
    slice x3 -> x2, local copies, waits for them, and re-layouts: 5.11 us -> 2.06 us  [the longest x1 2.05 us: body(): everyone[:, :columns * query_count]]
    unnamed x8 -> x6, local copies, waits for them, and re-layouts: 1.7 us -> 4.47 us
    all_to_all x1, starting transfers between devices: 3.28 us -> 5.53 us  [body(): lax.all_to_all(answers.reshape(device_count, capacity, list_size), AXES,...]
  transfers between devices with their start and end apart: 2 -> 1, of which waited for: 2 -> 1; matrix products, arithmetic and copies ran while one was open for 5% -> 0% of each run, Pallas kernels for 0% -> 0%
where the time goes in v2:
time: 114 us
  Pallas kernels  32.3 us (28%)
  local copies, waits for them, and re-layouts  30 us (26%)
  waiting for transfers between devices  26.2 us (23%)
  matrix products  11.2 us (10%)
  other arithmetic  8.43 us (7%)
  starting transfers between devices  5.53 us (5%)
    pallas_call x1, Pallas kernels, gather_all(): pl.pallas_call(gather_kernel, out_shape=jax.ShapeDtypeStruct((device_coun...  32.3 us
    all_to_all x1, waiting for transfers between devices, body(): lax.all_to_all(answers.reshape(device_count, capacity, list_size), AXES,...  26.2 us
    dot_general x1, matrix products, body(): jnp.einsum('lcd,lvd->lcv', grouped, lists, preferred_element_type=jnp.flo...  8.82 us
    dot_general x1, other arithmetic, body(): jnp.einsum('lvd,lvd->lv', lists, lists, preferred_element_type=jnp.float32)  7.11 us
    gather x1, local copies, waits for them, and re-layouts, body(): grouped = rows[grouped_row].reshape(lists_here, list_capacity, width)  6.95 us
    all_to_all x1, starting transfers between devices, body(): lax.all_to_all(answers.reshape(device_count, capacity, list_size), AXES,...  5.53 us
    reshape x1, local copies, waits for them, and re-layouts, body(): everyone[:, :columns * query_count]  4.81 us
    gather x1, local copies, waits for them, and re-layouts, body(): answers = flat_dist[jnp.maximum(spot, 0)]  4.67 us
  transfers between devices with their start and end apart: 1, of which 1 were waited for; matrix products, arithmetic and copies ran while one was open for 0% of the time, Pallas kernels for 0%

profile of v2, /device:TPU:0, one launch (start us, length us, event | category | flops | bytes accessed | tf_op | source)
XLA Modules:
  0.0 113.9 jit_solution(16404360943564209053)
XLA Ops:
  0.0 0.0 copy-start
  0.0 0.9 copy.19
  0.9 0.1 reshape.430
  1.0 0.1 reshape.431
  1.1 0.1 reshape.429
  1.2 3.4 %gather_fusion = s32[512]{0:T(512)S(1)} fusion(s32[1024]{0:T(1024)} %param.9, s32[1024]{0:T(1024)S(1)} %pad_clamp_fusion.1), kind=kCustom, calls=%fused_computation | custom fusion | bytes 6144 | tf_op jit(solution)/shard_map/jit(_take)/gather | solution.py:117
  4.6 0.3 fusion.7
  4.9 0.1 pad_maximum_fusion.1
  5.0 0.3 fusion.8
  5.3 0.1 slice.38
  5.4 0.1 copy.22
  5.5 0.1 broadcast_in_dim.64
  5.6 0.1 copy.23
  5.7 0.1 slice.24
  5.8 0.0 copy-done
  5.8 1.2 %convolution_convert_fusion = bf16[64,768]{1,0:T(8,128)(2,1)S(1)} fusion(bf16[64,768]{1,0:T(8,128)(2,1)} %param.5, bf16[768,768]{1,0:T(8,128)(2,1)S(1)} %copy-done), kind=kOutput, calls=%fused_computation.16 | convolution fusion | flops 75546624 | bytes 1376256 | tf_op jit(solution)/shard_map/dot_general | solution.py:114
  7.0 0.1 reshape.427
  7.2 32.3 %shard_map.55 = bf16[32,400,128]{2,1,0:T(8,128)(2,1)S(1)} custom-call(bf16[400,128]{1,0:T(8,128)(2,1)S(1)} %pad_maximum_fusion.mine_ref), custom_call_target="tpu_custom_call" | custom-call | tf_op jit(solution)/shard_map/pallas_call | solution.py:88
  39.5 2.0 %slice.25 = bf16[32,384,128]{2,1,0:T(8,128)(2,1)} slice(bf16[32,400,128]{2,1,0:T(8,128)(2,1)S(1)} %shard_map.55), slice={[0:32], [0:384], [0:128]} | slice | bytes 6291456 | tf_op jit(solution)/shard_map/slice | solution.py:144
  41.6 0.2 reshape_reshape.3
  41.9 0.1 reshape_squeeze.6
  42.0 0.5 fusion.6
  42.6 7.1 %fusion = f32[32,256]{1,0:T(8,128)S(1)} fusion(bf16[32,256,768]{2,1,0:T(8,128)(2,1)} %param.7), kind=kLoop, calls=%fused_computation.5 | loop fusion | flops 18866176 | bytes 12615680 | tf_op jit(solution)/shard_map/lvd,lvd->lv/dot_general | solution.py:171
  49.7 0.1 ge.54
  49.8 0.1 mul.91
  49.9 0.1 reshape_squeeze.7
  50.0 0.6 select_reduce_fusion
  50.7 4.8 %copy.24 = bf16[32,6,64,128]{3,1,2,0:T(8,128)(2,1)S(1)} copy(bf16[32,6,64,128]{3,2,1,0:T(8,128)(2,1)} %bitcast.49) | data formatting | bytes 6291456 | tf_op jit(solution)/shard_map/reshape | solution.py:144
  55.5 2.5 %copy.40 = bf16[256,8,6,128]{3,1,2,0:T(8,128)(2,1)} copy(bf16[256,8,6,128]{3,2,1,0:T(8,128)(2,1)S(1)} %bitcast.46) | data formatting | bytes 6291456
  57.9 6.9 %gather_fusion.1 = bf16[1024,768]{1,0:T(8,128)(2,1)S(1)} fusion(bf16[2048,768]{1,0:T(8,128)(2,1)} %bitcast.44, s32[1024]{0:T(1024)S(1)} %broadcast_clamp_fusion), kind=kCustom, calls=%fused_computation.1 | custom fusion | bytes 3149824 | tf_op jit(solution)/shard_map/gather | solution.py:168
  64.9 0.0 copy-start.1
  64.9 1.1 %copy-done.1 = bf16[1024,768]{1,0:T(8,128)(2,1)} copy-done((bf16[1024,768]{1,0:T(8,128)(2,1)}, bf16[1024,768]{1,0:T(8,128)(2,1)S(1)}, u32[]{:S(2)}) %copy-start.1) | copy-done | bytes 1572888
  66.0 0.4 fusion.2
  66.4 8.8 %fusion.4 = f32[32,32,256]{2,1,0:T(8,128)S(1)} fusion(bf16[32,32,768]{2,1,0:T(8,128)(2,1)} %bitcast.48, bf16[32,256,768]{2,1,0:T(8,128)(2,1)} %param.7, f32[32,256]{1,0:T(8,128)S(1)} %fusion, f32[32,32]{1,0:T(8,128)S(1)} %fusion.2), kind=kOutput, calls=%fused_computation.15 | convolution fusion | flops 403701760 | bytes 15241216 | tf_op jit(solution)/shard_map/lcd,lvd->lcv/dot_general | solution.py:170
  75.2 4.7 %gather_fusion.2 = f32[1024,256]{1,0:T(8,128)} fusion(f32[1024,256]{1,0:T(8,128)S(1)} %bitcast.43, s32[1024]{0:T(1024)S(1)} %broadcast_clamp_fusion.1), kind=kCustom, calls=%fused_computation.2 | custom fusion | bytes 2101248 | tf_op jit(solution)/shard_map/gather | solution.py:175
  79.9 5.5 %all-to-all-start = ((f32[32,32,256]{2,1,0:T(8,128)}), f32[32,32,256]{2,1,0:T(8,128)S(1)}, u32[]{:S(2)}, u32[]{:S(2)}) async-start(f32[32,32,256]{2,1,0:T(8,128)} %bitcast.15), calls=%async_computation | async-start | bytes 2097152 | tf_op jit(solution)/shard_map/all_to_all | solution.py:176
  85.5 26.2 %all-to-all-done = f32[32,32,256]{2,1,0:T(8,128)S(1)} async-done(((f32[32,32,256]{2,1,0:T(8,128)}), f32[32,32,256]{2,1,0:T(8,128)S(1)}, u32[]{:S(2)}, u32[]{:S(2)}) %all-to-all-start) | async-done | bytes 1048608 | tf_op jit(solution)/shard_map/all_to_all | solution.py:176
  111.7 2.2 %gather_fusion.3 = f32[512,256]{1,0:T(8,128)} fusion(f32[1024,256]{1,0:T(8,128)S(1)} %bitcast.45, s32[1024]{0:T(1024)S(1)} %pad_clamp_fusion), kind=kCustom, calls=%fused_computation.3 | custom fusion | bytes 1050624 | tf_op jit(solution)/shard_map/gather | solution.py:184
  (27 shorter events, 0.3 us)
Async XLA Ops:
  0.0 5.8 %copy-start = (bf16[768,768]{1,0:T(8,128)(2,1)S(1)}, bf16[768,768]{1,0:T(8,128)(2,1)}, u32[]{:S(2)}) copy-start(bf16[768,768]{1,0:T(8,128)(2,1)} %param.6) | copy-start | bytes 3538948
  64.9 1.2 %copy-start.1 = (bf16[1024,768]{1,0:T(8,128)(2,1)}, bf16[1024,768]{1,0:T(8,128)(2,1)S(1)}, u32[]{:S(2)}) copy-start(bf16[1024,768]{1,0:T(8,128)(2,1)S(1)} %gather_fusion.1) | copy-start | bytes 4718596
  79.9 31.8 %all-to-all-start = ((f32[32,32,256]{2,1,0:T(8,128)}), f32[32,32,256]{2,1,0:T(8,128)S(1)}, u32[]{:S(2)}, u32[]{:S(2)}) async-start(f32[32,32,256]{2,1,0:T(8,128)} %bitcast.15), calls=%async_computation | async-start | bytes 2097152 | tf_op jit(solution)/shard_map/all_to_all | solution.py:176

commit v3 on v2

--- a/solution.py
+++ b/solution.py
@@ -100,6 +100,95 @@
     )(block)
 
 
+def select_kernel(queries, width, row_ref, all_ref, out_ref):
+    devices = all_ref.shape[0]
+    count = out_ref.shape[0]
+    numbers = lax.broadcasted_iota(jnp.int32, (count, devices * queries), 1)
+    pick = (numbers == row_ref[...]).astype(jnp.float32).astype(jnp.bfloat16)
+    for j in range(width // LANES):
+        part = all_ref[:, j * queries : (j + 1) * queries, :].reshape(devices * queries, LANES)
+        out_ref[:, j * LANES : (j + 1) * LANES] = jnp.dot(
+            pick, part, preferred_element_type=jnp.float32
+        ).astype(jnp.bfloat16)
+
+
+def select_rows(everyone, row_of, queries, width):
+    slots = row_of.shape[0]
+    block = min(256, slots)
+    return pl.pallas_call(
+        lambda *refs: select_kernel(queries, width, *refs),
+        grid=(slots // block,),
+        out_shape=jax.ShapeDtypeStruct((slots, width), jnp.bfloat16),
+        in_specs=[
+            pl.BlockSpec((block, 1), lambda i: (i, 0)),
+            pl.BlockSpec(memory_space=pltpu.VMEM),
+        ],
+        out_specs=pl.BlockSpec((block, width), lambda i: (i, 0)),
+        compiler_params=pltpu.CompilerParams(vmem_limit_bytes=48 * 2**20),
+    )(row_of[:, None], everyone)
+
+
+def exchange_kernel(device_count, owner_count, out_ref, in_ref, send_sem, recv_sem):
+    me = lax.axis_index("grp") * owner_count + lax.axis_index("own")
+
+    def at(k):
+        other = lax.rem(me + k, device_count)
+        return other, (other // owner_count, lax.rem(other, owner_count))
+
+    barrier = pltpu.get_barrier_semaphore()
+
+    @pl.loop(1, device_count)
+    def _(k):
+        pl.semaphore_signal(
+            barrier, inc=1, device_id=at(k)[1], device_id_type=pl.DeviceIdType.MESH
+        )
+
+    pl.semaphore_wait(barrier, device_count - 1)
+
+    def describe(k, block):
+        other, where = at(k)
+        return pltpu.make_async_remote_copy(
+            src_ref=out_ref.at[other],
+            dst_ref=in_ref.at[block],
+            send_sem=send_sem.at[k],
+            recv_sem=recv_sem.at[block],
+            device_id=where,
+            device_id_type=pl.DeviceIdType.MESH,
+        )
+
+    @pl.loop(1, device_count)
+    def _(k):
+        describe(k, me).start()
+
+    in_ref[me] = out_ref[me]
+
+    @pl.loop(1, device_count)
+    def _(k):
+        describe(k, at(k)[0]).wait_recv()
+
+    @pl.loop(1, device_count)
+    def _(k):
+        describe(k, me).wait_send()
+
+
+def exchange(blocks):
+    owner_count = lax.axis_size("own")
+    device_count = blocks.shape[0]
+    return pl.pallas_call(
+        lambda *refs: exchange_kernel(device_count, owner_count, *refs),
+        out_shape=jax.ShapeDtypeStruct(blocks.shape, blocks.dtype),
+        in_specs=[pl.BlockSpec(memory_space=pltpu.VMEM)],
+        out_specs=pl.BlockSpec(memory_space=pltpu.VMEM),
+        scratch_shapes=[
+            pltpu.SemaphoreType.DMA((device_count,)),
+            pltpu.SemaphoreType.DMA((device_count,)),
+        ],
+        compiler_params=pltpu.CompilerParams(
+            collective_id=1, has_side_effects=True, vmem_limit_bytes=16 * 2**20
+        ),
+    )(blocks)
+
+
 def body(queries, projection, lists, probes, owner_map):
     query_count, width = queries.shape
     probe_count = probes.shape[1]
@@ -141,10 +230,6 @@
     stacked = stacked.reshape(columns * query_count, LANES)
 
     everyone = gather_all(jnp.concatenate([stacked, table], axis=0))
-    rows = everyone[:, : columns * query_count].reshape(
-        device_count, columns, query_count, LANES
-    )
-    rows = rows.transpose(0, 2, 1, 3).reshape(device_count * query_count, width)
     tables = everyone[:, columns * query_count :].reshape(device_count, -1)[:, : 2 * slots]
     tables = tables.reshape(device_count, 2, device_count, capacity)
     mine = lax.dynamic_index_in_dim(tables, me, axis=2, keepdims=False).astype(jnp.int32)
@@ -165,22 +250,46 @@
     spot = jnp.where(valid, asked_list * list_capacity + order, -1)
     hit = spot[:, None] == jnp.arange(lists_here * list_capacity, dtype=jnp.int32)[None, :]
     grouped_row = jnp.sum(jnp.where(hit, row_of[:, None], 0), axis=0)
-    grouped = rows[grouped_row].reshape(lists_here, list_capacity, width)
+    grouped = select_rows(everyone, grouped_row, query_count, width)
+    grouped = grouped.reshape(lists_here, list_capacity, width)
 
     dots = jnp.einsum("lcd,lvd->lcv", grouped, lists, preferred_element_type=jnp.float32)
     vec_norm = jnp.einsum("lvd,lvd->lv", lists, lists, preferred_element_type=jnp.float32)
     row_norm = jnp.einsum("lcd,lcd->lc", grouped, grouped, preferred_element_type=jnp.float32)
     distance = (row_norm[:, :, None] + vec_norm[:, None, :] - 2.0 * dots) / width
     flat_dist = distance.reshape(lists_here * list_capacity, list_size)
-    answers = flat_dist[jnp.maximum(spot, 0)]
-    returned = lax.all_to_all(
-        answers.reshape(device_count, capacity, list_size),
-        AXES,
-        split_axis=0,
-        concat_axis=0,
-        tiled=True,
-    )
-    returned = returned.reshape(slots, list_size)
+    largest = jnp.max(jnp.abs(flat_dist), axis=1, keepdims=True)
+    power = jnp.clip(jnp.ceil(jnp.log2(largest) + 1e-3), -120.0, 120.0)
+    codes = jnp.round(jnp.maximum(flat_dist, 0.0) * (65535.0 * jnp.exp2(-power))) - 32768.0
+    codes = jnp.clip(codes, -32768.0, 32767.0)
+    coded = jnp.concatenate(
+        [codes, jnp.broadcast_to(power, (power.shape[0], LANES))], axis=1
+    )[jnp.maximum(spot, 0)]
+    answer_rows = capacity * list_size // LANES
+    power_rows = -(-capacity // (16 * LANES)) * 16
+    powers = jnp.pad(
+        coded[:, list_size].reshape(device_count, capacity),
+        ((0, 0), (0, power_rows * LANES - capacity)),
+    )
+    blocks = jnp.concatenate(
+        [
+            coded[:, :list_size]
+            .reshape(device_count, capacity, list_size // LANES, LANES)
+            .transpose(0, 2, 1, 3)
+            .reshape(device_count, answer_rows, LANES),
+            powers.reshape(device_count, power_rows, LANES),
+        ],
+        axis=1,
+    ).astype(jnp.int16)
+    got = exchange(blocks).astype(jnp.float32)
+    powers = got[:, answer_rows:].reshape(device_count, -1)[:, :capacity].reshape(slots, 1)
+    returned = (
+        got[:, :answer_rows]
+        .reshape(device_count, list_size // LANES, capacity, LANES)
+        .transpose(0, 2, 1, 3)
+        .reshape(slots, list_size)
+    )
+    returned = (returned + 32768.0) * (jnp.exp2(powers) / 65535.0)
     return returned[position].reshape(query_count, probe_count, list_size)
 
 

time: 114 us -> 103 us (0.904)
  the two profiles are of different devices: /device:TPU:0 before, /device:TPU:11 now
where the time goes in v3:
time: 103 us; the launch traced here: 102 us
  Pallas kernels  60.4 us (59%)
  local copies, waits for them, and re-layouts  18.5 us (18%)
  other arithmetic  12.2 us (12%)
  matrix products  10.8 us (10%)
    pallas_call x1, Pallas kernels, gather_all(): pl.pallas_call(gather_kernel, out_shape=jax.ShapeDtypeStruct((device_coun...  32 us
    pallas_call x1, Pallas kernels, exchange(): pl.pallas_call(lambda *refs: exchange_kernel(device_count, owner_count, *...  20.9 us
    dot_general x1, matrix products, body(): jnp.einsum('lcd,lvd->lcv', grouped, lists, preferred_element_type=jnp.flo...  9.36 us
    pallas_call x1, Pallas kernels, select_rows(): pl.pallas_call(lambda *refs: select_kernel(queries, width, *refs), grid=(...  7.44 us
    dot_general x1, other arithmetic, body(): jnp.einsum('lvd,lvd->lv', lists, lists, preferred_element_type=jnp.float32)  7.11 us
    gather x1, local copies, waits for them, and re-layouts, body(): jnp.concatenate([codes, jnp.broadcast_to(power, (power.shape[0], LANES))]...  4.77 us
    unnamed x12, local copies, waits for them, and re-layouts  4.61 us
    gather x1, local copies, waits for them, and re-layouts, body(): stored = jnp.take(owner_map, probes.reshape(-1))  3.37 us

profile of v3, /device:TPU:11, one launch (start us, length us, event | category | flops | bytes accessed | tf_op | source)
XLA Modules:
  0.0 102.3 jit_solution(3397476441543608638)
XLA Ops:
  0.0 0.0 copy-start
  0.0 0.0 copy-start.3
  0.0 0.9 copy.22
  0.9 0.1 reshape.477
  1.0 3.4 %gather_fusion = s32[512]{0:T(512)S(1)} fusion(s32[1024]{0:T(1024)} %param.9, s32[1024]{0:T(1024)S(1)} %pad_clamp_fusion.1), kind=kCustom, calls=%fused_computation | custom fusion | bytes 6144 | tf_op jit(solution)/shard_map/jit(_take)/gather | solution.py:206
  4.4 0.1 reshape.478
  4.5 0.1 pad_maximum_fusion.2
  4.6 0.1 reshape.476
  4.7 0.3 fusion.7
  5.0 0.3 fusion.11
  5.3 0.1 slice.54
  5.4 0.1 copy.26
  5.5 0.1 slice.38
  5.6 0.1 copy.25
  5.7 0.1 broadcast_in_dim.72
  5.8 0.0 copy-done
  5.8 0.0 copy-done.3
  5.8 0.3 convolution_convert_fusion
  6.2 0.1 reshape.474
  6.3 32.0 %shard_map.55.refs_1_ = bf16[32,400,128]{2,1,0:T(8,128)(2,1)S(1)} custom-call(bf16[400,128]{1,0:T(8,128)(2,1)S(1)} %pad_maximum_fusion.1.mine_ref), custom_call_target="tpu_custom_call" | custom-call | tf_op jit(solution)/shard_map/pallas_call | solution.py:88
  38.4 0.0 copy-start.1
  38.4 1.7 %copy-done.1 = bf16[32,400,128]{2,1,0:T(8,128)(2,1)} copy-done((bf16[32,400,128]{2,1,0:T(8,128)(2,1)}, bf16[32,400,128]{2,1,0:T(8,128)(2,1)S(1)}, u32[]{:S(2)}) %copy-start.1) | copy-done | bytes 3276824
  40.0 0.2 reshape_reshape.3
  40.4 0.1 reshape_squeeze.10
  40.5 0.5 fusion.6
  41.0 0.1 mul.118
  41.1 0.1 ge.54
  41.2 0.1 reshape_squeeze.11
  41.3 0.6 select_reduce_fusion
  42.0 0.2 copy.28.refs_0_
  42.2 0.0 copy-start.2
  42.2 1.9 %copy-done.2 = bf16[32,400,128]{2,1,0:T(8,128)(2,1)S(1)} copy-done((bf16[32,400,128]{2,1,0:T(8,128)(2,1)S(1)}, bf16[32,400,128]{2,1,0:T(8,128)(2,1)}, u32[]{:S(2)}) %copy-start.2) | copy-done | bytes 3276824
  44.1 7.4 %shard_map.56 = bf16[1024,768]{1,0:T(8,128)(2,1)S(1)} custom-call(s32[1024,1]{1,0:T(8,128)S(1)} %copy.28.refs_0_, bf16[32,400,128]{2,1,0:T(8,128)(2,1)S(1)} %copy-done.2), custom_call_target="tpu_custom_call" | custom-call | tf_op jit(solution)/shard_map/pallas_call | solution.py:118
  51.6 0.4 fusion.2
  52.0 7.1 %fusion = f32[32,256]{1,0:T(8,128)S(1)} fusion(bf16[32,256,768]{2,1,0:T(8,128)(2,1)} %param.7), kind=kLoop, calls=%fused_computation.4 | loop fusion | flops 18866176 | bytes 12615680 | tf_op jit(solution)/shard_map/lvd,lvd->lv/dot_general | solution.py:257
  59.1 9.4 %broadcast_maximum_fusion = (f32[32,32,256]{2,1,0:T(8,128)}, f32[32,32]{1,0:T(8,128)S(1)}) fusion(bf16[32,32,768]{2,1,0:T(8,128)(2,1)S(1)} %bitcast.58, bf16[32,256,768]{2,1,0:T(8,128)(2,1)} %param.7, f32[32,256]{1,0:T(8,128)S(1)} %fusion, f32[32,32]{1,0:T(8,128)S(1)} %fusion.2), kind=kOutput, calls=%fused_computation.29 | convolution fusion | flops 404487168 | bytes 15245312 | tf_op jit(solution)/shard_map/lcd,lvd->lcv/dot_general | solution.py:256
  68.4 0.1 reshape.488
  68.5 1.5 %fusion.10 = f32[1024,256]{1,0:T(8,128)S(1)} fusion(f32[32,32,256]{2,1,0:T(8,128)} %get-tuple-element.5, f32[1024]{0:T(1024)S(1)} %exponential_multiply_fusion), kind=kLoop, calls=%fused_computation.25 | loop fusion | flops 1048576 | bytes 2101248 | tf_op jit(solution)/shard_map/jit(clip)/min | solution.py:264
  70.0 0.2 broadcast_in_dim.78
  70.2 0.1 pad_maximum_fusion
  70.3 4.8 %gather_fusion.1 = f32[1024,384]{1,0:T(8,128)} fusion(f32[1024,384]{1,0:T(8,128)S(1)} %pad_maximum_fusion, s32[1024]{0:T(1024)S(1)} %broadcast_clamp_fusion), kind=kCustom, calls=%fused_computation.1 | custom fusion | bytes 3149824 | tf_op jit(solution)/shard_map/gather | solution.py:265
  75.1 1.7 %convert.24 = s16[1024,384]{1,0:T(8,128)(2,1)S(1)} convert(f32[1024,384]{1,0:T(8,128)} %gather_fusion.1) | non-fusion elementwise | flops 393216 | bytes 2359296 | tf_op jit(solution)/shard_map/convert.11
  76.8 0.1 reshape.480
  76.9 0.1 copy.29
  77.0 0.2 slice_reduce_fusion
  77.3 0.1 reshape_squeeze.12
  77.5 20.9 %shard_map.57 = s16[32,80,128]{2,1,0:T(8,128)(2,1)S(1)} custom-call(s16[32,80,128]{2,1,0:T(8,128)(2,1)S(1)} %pad_add_fusion.refs_0_), custom_call_target="tpu_custom_call" | custom-call | tf_op jit(solution)/shard_map/pallas_call | solution.py:177
  98.4 0.2 convert_element_type.90
  98.6 0.1 slice_add_fusion
  98.7 0.8 copy.30
  99.6 0.1 copy.48
  99.7 0.1 div.56
  99.8 0.2 bitcast_multiply_fusion
  100.0 2.2 %gather_fusion.2 = f32[512,256]{1,0:T(8,128)} fusion(f32[1024,256]{1,0:T(8,128)S(1)} %bitcast_multiply_fusion, s32[1024]{0:T(1024)S(1)} %pad_clamp_fusion), kind=kCustom, calls=%fused_computation.2 | custom fusion | bytes 1050624 | tf_op jit(solution)/shard_map/gather | solution.py:293
  (33 shorter events, 0.5 us)
Async XLA Ops:
  0.0 5.8 %copy-start = (bf16[768,768]{1,0:T(8,128)(2,1)S(1)}, bf16[768,768]{1,0:T(8,128)(2,1)}, u32[]{:S(2)}) copy-start(bf16[768,768]{1,0:T(8,128)(2,1)} %param.6) | copy-start | bytes 3538948
  0.0 5.8 %copy-start.3 = (bf16[64,768]{1,0:T(8,128)(2,1)S(1)}, bf16[64,768]{1,0:T(8,128)(2,1)}, u32[]{:S(2)}) copy-start(bf16[64,768]{1,0:T(8,128)(2,1)} %param.5) | copy-start | bytes 294916
  38.4 1.7 %copy-start.1 = (bf16[32,400,128]{2,1,0:T(8,128)(2,1)}, bf16[32,400,128]{2,1,0:T(8,128)(2,1)S(1)}, u32[]{:S(2)}) copy-start(bf16[32,400,128]{2,1,0:T(8,128)(2,1)S(1)} %shard_map.55.refs_1_) | copy-start | bytes 9830404
  42.2 1.9 %copy-start.2 = (bf16[32,400,128]{2,1,0:T(8,128)(2,1)S(1)}, bf16[32,400,128]{2,1,0:T(8,128)(2,1)}, u32[]{:S(2)}) copy-start(bf16[32,400,128]{2,1,0:T(8,128)(2,1)} %copy-done.1) | copy-start | bytes 9830404

commit v4 on v3

--- a/solution.py
+++ b/solution.py
@@ -7,6 +7,8 @@
 
 AXES = ("grp", "own")
 LANES = 128
+LOG2E = 1.4426950408889634
+LN2 = 0.6931471805599453
 
 
 def gather_kernel(mine_ref, all_ref, send_sem, recv_sem):
@@ -128,6 +130,76 @@
     )(row_of[:, None], everyone)
 
 
+def score_kernel(blocks, rows_ref, lists_ref, spot_ref, out_ref, held):
+    step = pl.program_id(0)
+    count, list_size, width = lists_ref.shape
+    capacity = rows_ref.shape[0] // count
+    for n in range(count):
+        rows = rows_ref[n * capacity : (n + 1) * capacity, :]
+        dots = lax.dot_general(
+            rows, lists_ref[n], (((1,), (1,)), ((), ())), preferred_element_type=jnp.float32
+        )
+        rows_f = rows.astype(jnp.float32)
+        row_norm = jnp.sum(rows_f * rows_f, axis=1, keepdims=True)
+        partial = None
+        for j in range(width // LANES):
+            part = lists_ref[n, :, j * LANES : (j + 1) * LANES].astype(jnp.float32)
+            partial = part * part if partial is None else partial + part * part
+        vec_norm = jnp.sum(partial.T, axis=0, keepdims=True)
+        distance = jnp.maximum((row_norm + vec_norm - 2.0 * dots) / width, 0.0)
+        largest = jnp.maximum(jnp.max(distance, axis=1, keepdims=True), 1e-30)
+        power = jnp.clip(jnp.ceil(jnp.log(largest) * LOG2E + 1e-3), -100.0, 120.0)
+        code = jnp.clip(jnp.round(distance * (65535.0 * jnp.exp(power * -LN2))), 0.0, 65535.0)
+        high = jnp.floor(code * (1.0 / 256.0))
+        low = code - high * 256.0
+        place = pl.ds(pl.multiple_of((step * count + n) * capacity, 16), capacity)
+        held[place, :list_size] = high.astype(jnp.bfloat16)
+        held[place, list_size : 2 * list_size] = low.astype(jnp.bfloat16)
+        held[place, 2 * list_size :] = jnp.broadcast_to(power, (capacity, LANES)).astype(
+            jnp.bfloat16
+        )
+
+    @pl.when(step == pl.num_programs(0) - 1)
+    def _():
+        slots = held.shape[0]
+        each = slots // blocks
+        numbers = lax.broadcasted_iota(jnp.int32, (slots, slots), 1)
+        pick = (numbers == spot_ref[...]).astype(jnp.float32).astype(jnp.bfloat16)
+        got = jnp.dot(pick, held[...], preferred_element_type=jnp.float32)
+        code = got[:, :list_size] * 256.0 + got[:, list_size : 2 * list_size] - 32768.0
+        parts = [
+            code[:, h * LANES : (h + 1) * LANES].reshape(blocks, each, LANES)
+            for h in range(list_size // LANES)
+        ]
+        powers = got[:, 2 * list_size :].reshape(blocks, each, LANES)
+        slot = lax.broadcasted_iota(jnp.int32, powers.shape, 1)
+        lane = lax.broadcasted_iota(jnp.int32, powers.shape, 2)
+        powers = jnp.sum(jnp.where(slot == lane, powers, 0.0), axis=1, keepdims=True)
+        parts.append(jnp.broadcast_to(powers, (blocks, 16, LANES)))
+        whole = jnp.concatenate(parts, axis=1)
+        out_ref[...] = whole.astype(jnp.int32).astype(jnp.int16)
+
+
+def score(grouped, lists, spot, blocks):
+    list_count, list_size, width = lists.shape
+    slots = grouped.shape[0]
+    count = 4
+    out_rows = (slots // blocks) * list_size // LANES + 16
+    return pl.pallas_call(
+        lambda *refs: score_kernel(blocks, *refs),
+        grid=(list_count // count,),
+        out_shape=jax.ShapeDtypeStruct((blocks, out_rows, LANES), jnp.int16),
+        in_specs=[
+            pl.BlockSpec((slots // list_count * count, width), lambda i: (i, 0)),
+            pl.BlockSpec((count, list_size, width), lambda i: (i, 0, 0)),
+            pl.BlockSpec((slots, 1), lambda i: (0, 0)),
+        ],
+        out_specs=pl.BlockSpec((blocks, out_rows, LANES), lambda i: (0, 0, 0)),
+        scratch_shapes=[pltpu.VMEM((slots, 2 * list_size + LANES), jnp.bfloat16)],
+        compiler_params=pltpu.CompilerParams(vmem_limit_bytes=40 * 2**20),
+    )(grouped, lists, spot[:, None])
+
+
 def exchange_kernel(device_count, owner_count, out_ref, in_ref, send_sem, recv_sem):
     me = lax.axis_index("grp") * owner_count + lax.axis_index("own")
 
@@ -251,36 +323,8 @@
     hit = spot[:, None] == jnp.arange(lists_here * list_capacity, dtype=jnp.int32)[None, :]
     grouped_row = jnp.sum(jnp.where(hit, row_of[:, None], 0), axis=0)
     grouped = select_rows(everyone, grouped_row, query_count, width)
-    grouped = grouped.reshape(lists_here, list_capacity, width)
-
-    dots = jnp.einsum("lcd,lvd->lcv", grouped, lists, preferred_element_type=jnp.float32)
-    vec_norm = jnp.einsum("lvd,lvd->lv", lists, lists, preferred_element_type=jnp.float32)
-    row_norm = jnp.einsum("lcd,lcd->lc", grouped, grouped, preferred_element_type=jnp.float32)
-    distance = (row_norm[:, :, None] + vec_norm[:, None, :] - 2.0 * dots) / width
-    flat_dist = distance.reshape(lists_here * list_capacity, list_size)
-    largest = jnp.max(jnp.abs(flat_dist), axis=1, keepdims=True)
-    power = jnp.clip(jnp.ceil(jnp.log2(largest) + 1e-3), -120.0, 120.0)
-    codes = jnp.round(jnp.maximum(flat_dist, 0.0) * (65535.0 * jnp.exp2(-power))) - 32768.0
-    codes = jnp.clip(codes, -32768.0, 32767.0)
-    coded = jnp.concatenate(
-        [codes, jnp.broadcast_to(power, (power.shape[0], LANES))], axis=1
-    )[jnp.maximum(spot, 0)]
+    blocks = score(grouped, lists, spot, device_count)
     answer_rows = capacity * list_size // LANES
-    power_rows = -(-capacity // (16 * LANES)) * 16
-    powers = jnp.pad(
-        coded[:, list_size].reshape(device_count, capacity),
-        ((0, 0), (0, power_rows * LANES - capacity)),
-    )
-    blocks = jnp.concatenate(
-        [
-            coded[:, :list_size]
-            .reshape(device_count, capacity, list_size // LANES, LANES)
-            .transpose(0, 2, 1, 3)
-            .reshape(device_count, answer_rows, LANES),
-            powers.reshape(device_count, power_rows, LANES),
-        ],
-        axis=1,
-    ).astype(jnp.int16)
     got = exchange(blocks).astype(jnp.float32)
     powers = got[:, answer_rows:].reshape(device_count, -1)[:, :capacity].reshape(slots, 1)
     returned = (

time: 103 us -> 92.4 us (0.90)
  Pallas kernels: 60.4 us -> 72.1 us
  other arithmetic: 12.2 us -> 2.56 us
  matrix products: 10.8 us -> 2.32 us
  local copies, waits for them, and re-layouts: 18.5 us -> 14.8 us
    pallas_call x0 -> x1, Pallas kernels: none -> 11.7 us  [score(): pl.pallas_call(lambda *refs: score_kernel(blocks, *refs), grid=(list_coun...]
    dot_general x1 -> x0, matrix products: 9.36 us -> none  [body(): jnp.einsum('lcd,lvd->lcv', grouped, lists, preferred_element_type=jnp.flo...]
    dot_general x2 -> x0, other arithmetic: 7.48 us -> none  [the longest x1 7.11 us: body(): jnp.einsum('lvd,lvd->lv', lists, lists, preferred_element_type=jnp.float32)]
    gather x1 -> x0, local copies, waits for them, and re-layouts: 4.77 us -> none  [body(): jnp.concatenate([codes, jnp.broadcast_to(power, (power.shape[0], LANES))]...]
    another operation x2 -> x1, other arithmetic: 1.68 us -> 0.03 us
    min x2 -> x0, other arithmetic: 1.48 us -> none  [the longest x1 1.47 us: body(): codes = jnp.clip(codes, -32768.0, 32767.0)]
    select_n x1 -> x2, other arithmetic: 0.01 us -> 1.12 us  [body(): spot = jnp.where(valid, asked_list * list_capacity + order, -1)]
    unnamed x12 -> x8, local copies, waits for them, and re-layouts: 4.61 us -> 4.56 us
where the time goes in v4:
time: 92.4 us; the launch traced here: 92 us
  Pallas kernels  72.1 us (78%)
  local copies, waits for them, and re-layouts  14.8 us (16%)
  other arithmetic  2.56 us (3%)
  matrix products  2.32 us (3%)
    pallas_call x1, Pallas kernels, gather_all(): pl.pallas_call(gather_kernel, out_shape=jax.ShapeDtypeStruct((device_coun...  32 us
    pallas_call x1, Pallas kernels, exchange(): pl.pallas_call(lambda *refs: exchange_kernel(device_count, owner_count, *...  20.9 us
    pallas_call x1, Pallas kernels, score(): pl.pallas_call(lambda *refs: score_kernel(blocks, *refs), grid=(list_coun...  11.7 us
    pallas_call x1, Pallas kernels, select_rows(): pl.pallas_call(lambda *refs: select_kernel(queries, width, *refs), grid=(...  7.44 us
    unnamed x8, local copies, waits for them, and re-layouts  4.56 us
    gather x1, local copies, waits for them, and re-layouts, body(): stored = jnp.take(owner_map, probes.reshape(-1))  3.37 us
    gather x1, local copies, waits for them, and re-layouts, body(): return returned[position].reshape(query_count, probe_count, list_size)  2.24 us

profile of v4, /device:TPU:11, one launch (start us, length us, event | category | flops | bytes accessed | tf_op | source)
XLA Modules:
  0.0 92.0 jit_solution(14158271243396748265)
XLA Ops:
  0.0 0.0 copy-start
  0.0 0.9 copy.24
  0.9 0.1 reshape.415
  1.0 3.4 %gather_fusion = s32[512]{0:T(512)S(1)} fusion(s32[1024]{0:T(1024)} %param.9, s32[1024]{0:T(1024)S(1)} %pad_clamp_fusion.1), kind=kCustom, calls=%fused_computation | custom fusion | bytes 6144 | tf_op jit(solution)/shard_map/jit(_take)/gather | solution.py:278
  4.4 0.1 reshape.416
  4.5 0.1 pad_maximum_fusion.1
  4.6 0.1 reshape.414
  4.7 0.3 fusion.3
  5.0 0.3 fusion.4
  5.3 0.1 copy.27
  5.4 0.1 broadcast_in_dim.64
  5.5 0.1 slice.42
  5.6 0.1 copy.28
  5.7 0.1 slice.30
  5.8 0.0 copy-done
  5.8 1.2 %convolution_convert_fusion = bf16[64,768]{1,0:T(8,128)(2,1)S(1)} fusion(bf16[64,768]{1,0:T(8,128)(2,1)} %param.5, bf16[768,768]{1,0:T(8,128)(2,1)S(1)} %copy-done), kind=kOutput, calls=%fused_computation.6 | convolution fusion | flops 75546624 | bytes 1376256 | tf_op jit(solution)/shard_map/dot_general | solution.py:275
  7.0 0.1 reshape.412
  7.2 32.0 %shard_map.55.refs_1_ = bf16[32,400,128]{2,1,0:T(8,128)(2,1)S(1)} custom-call(bf16[400,128]{1,0:T(8,128)(2,1)S(1)} %pad_maximum_fusion.mine_ref), custom_call_target="tpu_custom_call" | custom-call | tf_op jit(solution)/shard_map/pallas_call | solution.py:90
  39.2 0.0 copy-start.1
  39.2 1.7 %copy-done.1 = bf16[32,400,128]{2,1,0:T(8,128)(2,1)} copy-done((bf16[32,400,128]{2,1,0:T(8,128)(2,1)}, bf16[32,400,128]{2,1,0:T(8,128)(2,1)S(1)}, u32[]{:S(2)}) %copy-start.1) | copy-done | bytes 3276824
  40.9 0.2 reshape_reshape.3
  41.3 0.1 reshape_squeeze.7
  41.3 0.1 reshape_squeeze.6
  41.4 0.5 fusion.2
  42.0 0.7 select_reduce_fusion
  42.6 0.2 copy.30.refs_0_
  42.9 0.0 copy-start.2
  42.9 1.9 %copy-done.2 = bf16[32,400,128]{2,1,0:T(8,128)(2,1)S(1)} copy-done((bf16[32,400,128]{2,1,0:T(8,128)(2,1)S(1)}, bf16[32,400,128]{2,1,0:T(8,128)(2,1)}, u32[]{:S(2)}) %copy-start.2) | copy-done | bytes 3276824
  44.8 7.4 %shard_map.56.refs_0_ = bf16[1024,768]{1,0:T(8,128)(2,1)S(1)} custom-call(s32[1024,1]{1,0:T(8,128)S(1)} %copy.30.refs_0_, bf16[32,400,128]{2,1,0:T(8,128)(2,1)S(1)} %copy-done.2), custom_call_target="tpu_custom_call" | custom-call | tf_op jit(solution)/shard_map/pallas_call | solution.py:120
  52.3 0.6 ge.61
  52.9 0.5 mul.93
  53.4 1.0 %copy.32 = s32[1024,1]{1,0:T(8,128)} copy(s32[1024,1]{0,1:T(1,128)S(1)} %bitcast.49) | data formatting | bytes 8192 | tf_op jit(solution)/shard_map/convert_element_type | solution.py:320
  54.4 1.1 %add_select_fusion.refs_2_ = s32[1024,1]{1,0:T(8,128)S(1)} fusion(pred[1024,1]{1,0:T(8,128)(4,1)S(1)} %ge.61, s32[1024,1]{1,0:T(8,128)S(1)} %mul.93, s32[1024,1]{1,0:T(8,128)} %copy.32), kind=kLoop, calls=%fused_computation.14 | loop fusion | flops 2048 | bytes 13312 | tf_op jit(solution)/shard_map/jit(_where)/select_n | solution.py:322
  55.5 11.7 %shard_map.57.refs_0_ = s16[32,80,128]{2,1,0:T(8,128)(2,1)S(1)} custom-call(bf16[1024,768]{1,0:T(8,128)(2,1)S(1)} %shard_map.56.refs_0_, bf16[32,256,768]{2,1,0:T(8,128)(2,1)} %refs_1_.1, s32[1024,1]{1,0:T(8,128)S(1)} %add_select_fusion.refs_2_), custom_call_target="tpu_custom_call" | custom-call | tf_op jit(solution)/shard_map/pallas_call | solution.py:188
  67.3 20.9 %shard_map.58 = s16[32,80,128]{2,1,0:T(8,128)(2,1)S(1)} custom-call(s16[32,80,128]{2,1,0:T(8,128)(2,1)S(1)} %shard_map.57.refs_0_), custom_call_target="tpu_custom_call" | custom-call | tf_op jit(solution)/shard_map/pallas_call | solution.py:249
  88.2 0.2 convert_element_type.85
  88.4 0.1 slice_add_fusion
  88.5 0.8 copy.34
  89.4 0.1 copy.43
  89.5 0.1 div.52
  89.5 0.2 bitcast_multiply_fusion
  89.8 2.2 %gather_fusion.1 = f32[512,256]{1,0:T(8,128)} fusion(f32[1024,256]{1,0:T(8,128)S(1)} %bitcast_multiply_fusion, s32[1024]{0:T(1024)S(1)} %pad_clamp_fusion), kind=kCustom, calls=%fused_computation.1 | custom fusion | bytes 1050624 | tf_op jit(solution)/shard_map/gather | solution.py:337
  (25 shorter events, 0.3 us)
Async XLA Ops:
  0.0 5.8 %copy-start = (bf16[768,768]{1,0:T(8,128)(2,1)S(1)}, bf16[768,768]{1,0:T(8,128)(2,1)}, u32[]{:S(2)}) copy-start(bf16[768,768]{1,0:T(8,128)(2,1)} %param.6) | copy-start | bytes 3538948
  39.2 1.7 %copy-start.1 = (bf16[32,400,128]{2,1,0:T(8,128)(2,1)}, bf16[32,400,128]{2,1,0:T(8,128)(2,1)S(1)}, u32[]{:S(2)}) copy-start(bf16[32,400,128]{2,1,0:T(8,128)(2,1)S(1)} %shard_map.55.refs_1_) | copy-start | bytes 9830404
  42.9 1.9 %copy-start.2 = (bf16[32,400,128]{2,1,0:T(8,128)(2,1)S(1)}, bf16[32,400,128]{2,1,0:T(8,128)(2,1)}, u32[]{:S(2)}) copy-start(bf16[32,400,128]{2,1,0:T(8,128)(2,1)} %copy-done.1) | copy-start | bytes 9830404

commit v5 on v4

--- a/solution.py
+++ b/solution.py
@@ -31,53 +31,64 @@
     pl.semaphore_wait(barrier, 6)
 
     sent = []
-
-    def describe(src, block, peer, slot):
+    rows = mine_ref.shape[0]
+    middle = rows // 32 * 16
+    halves = ((0, middle), (middle, rows - middle))
+
+    def cut(ref, half):
+        return ref.at[pl.ds(*halves[half])]
+
+    def describe(src, block, half, peer, slot):
         return pltpu.make_async_remote_copy(
             src_ref=src,
-            dst_ref=all_ref.at[block],
+            dst_ref=cut(all_ref.at[block], half),
             send_sem=send_sem.at[slot],
-            recv_sem=recv_sem.at[block],
+            recv_sem=recv_sem.at[half, block],
             device_id=peer,
             device_id_type=pl.DeviceIdType.MESH,
         )
 
-    def send(src, block, peer):
-        copy = describe(src, block, peer, len(sent))
+    def send(src, block, half, peer):
+        copy = describe(src, block, half, peer, len(sent))
         copy.start()
         sent.append(copy)
 
-    def arrived(block):
-        describe(all_ref.at[block], block, sibling, 0).wait_recv()
-        return all_ref.at[block]
+    def arrived(block, half):
+        ref = cut(all_ref.at[block], half)
+        describe(ref, block, half, sibling, 0).wait_recv()
+        return ref
 
     me = number(z, x, y, c)
-    for peer in over_z + [over_x, over_y, sibling]:
-        send(mine_ref, me, peer)
+    for half in (0, 1):
+        for peer in over_z + [over_x, over_y, sibling]:
+            send(cut(mine_ref, half), me, half, peer)
     all_ref[me] = mine_ref[...]
     for k in (0, 1, 3, 2):
-        if k:
-            block = number(zs[k], x, y, c)
-            ref = arrived(block)
-            for peer in (over_x, over_y, sibling):
-                send(ref, block, peer)
-        block = number(zs[k], 1 - x, y, c)
-        ref = arrived(block)
-        if k % 2 == 1:
-            send(ref, block, over_y)
-        send(ref, block, sibling)
-        block = number(zs[k], x, 1 - y, c)
-        ref = arrived(block)
-        if k % 2 == 0:
-            send(ref, block, over_x)
-        send(ref, block, sibling)
+        for half in (0, 1):
+            if k:
+                block = number(zs[k], x, y, c)
+                ref = arrived(block, half)
+                for peer in (over_x, over_y, sibling):
+                    send(ref, block, half, peer)
+            block = number(zs[k], 1 - x, y, c)
+            ref = arrived(block, half)
+            if k % 2 == 1:
+                send(ref, block, half, over_y)
+            send(ref, block, half, sibling)
+            block = number(zs[k], x, 1 - y, c)
+            ref = arrived(block, half)
+            if k % 2 == 0:
+                send(ref, block, half, over_x)
+            send(ref, block, half, sibling)
     for k in (0, 1, 3, 2):
-        block = number(zs[k], 1 - x, 1 - y, c)
-        send(arrived(block), block, sibling)
+        for half in (0, 1):
+            block = number(zs[k], 1 - x, 1 - y, c)
+            send(arrived(block, half), block, half, sibling)
     for k in (0, 1, 3, 2):
-        for xx in (x, 1 - x):
-            for yy in (y, 1 - y):
-                arrived(number(zs[k], xx, yy, 1 - c))
+        for half in (0, 1):
+            for xx in (x, 1 - x):
+                for yy in (y, 1 - y):
+                    arrived(number(zs[k], xx, yy, 1 - c), half)
     for copy in sent:
         copy.wait_send()
 
@@ -93,8 +104,8 @@
         in_specs=[pl.BlockSpec(memory_space=pltpu.VMEM)],
         out_specs=pl.BlockSpec(memory_space=pltpu.VMEM),
         scratch_shapes=[
-            pltpu.SemaphoreType.DMA((device_count,)),
-            pltpu.SemaphoreType.DMA((device_count,)),
+            pltpu.SemaphoreType.DMA((2 * device_count,)),
+            pltpu.SemaphoreType.DMA((2, device_count)),
         ],
         compiler_params=pltpu.CompilerParams(
             collective_id=0, has_side_effects=True, vmem_limit_bytes=16 * 2**20
@@ -126,7 +137,9 @@
             pl.BlockSpec(memory_space=pltpu.VMEM),
         ],
         out_specs=pl.BlockSpec((block, width), lambda i: (i, 0)),
-        compiler_params=pltpu.CompilerParams(vmem_limit_bytes=48 * 2**20),
+        compiler_params=pltpu.CompilerParams(
+            vmem_limit_bytes=48 * 2**20
+        ),
     )(row_of[:, None], everyone)
 
 

time: 92.4 us -> 97 us (1.050)
  Pallas kernels: 72.1 us -> 76.7 us
    pallas_call x1, Pallas kernels: 32 us -> 38.1 us  [gather_all(): pl.pallas_call(gather_kernel, out_shape=jax.ShapeDtypeStruct((device_coun...]
    pallas_call x1, Pallas kernels: 20.9 us -> 19.4 us  [exchange(): pl.pallas_call(lambda *refs: exchange_kernel(device_count, owner_count, *...]
where the time goes in v5:
time: 97 us; the launch traced here: 96.7 us
  Pallas kernels  76.7 us (79%)
  local copies, waits for them, and re-layouts  14.8 us (15%)
  other arithmetic  2.56 us (3%)
  matrix products  2.32 us (2%)
    pallas_call x1, Pallas kernels, gather_all(): pl.pallas_call(gather_kernel, out_shape=jax.ShapeDtypeStruct((device_coun...  38.1 us
    pallas_call x1, Pallas kernels, exchange(): pl.pallas_call(lambda *refs: exchange_kernel(device_count, owner_count, *...  19.4 us
    pallas_call x1, Pallas kernels, score(): pl.pallas_call(lambda *refs: score_kernel(blocks, *refs), grid=(list_coun...  11.7 us
    pallas_call x1, Pallas kernels, select_rows(): pl.pallas_call(lambda *refs: select_kernel(queries, width, *refs), grid=(...  7.44 us
    unnamed x8, local copies, waits for them, and re-layouts  4.56 us
    gather x1, local copies, waits for them, and re-layouts, body(): stored = jnp.take(owner_map, probes.reshape(-1))  3.37 us
    gather x1, local copies, waits for them, and re-layouts, body(): return returned[position].reshape(query_count, probe_count, list_size)  2.24 us

profile of v5, /device:TPU:11, one launch (start us, length us, event | category | flops | bytes accessed | tf_op | source)
XLA Modules:
  0.0 96.7 jit_solution(15286251699388355074)
XLA Ops:
  0.0 0.0 copy-start
  0.0 0.9 copy.24
  0.9 0.1 reshape.415
  1.0 3.4 %gather_fusion = s32[512]{0:T(512)S(1)} fusion(s32[1024]{0:T(1024)} %param.9, s32[1024]{0:T(1024)S(1)} %pad_clamp_fusion.1), kind=kCustom, calls=%fused_computation | custom fusion | bytes 6144 | tf_op jit(solution)/shard_map/jit(_take)/gather | solution.py:291
  4.4 0.1 reshape.416
  4.5 0.1 pad_maximum_fusion.1
  4.6 0.1 reshape.414
  4.7 0.3 fusion.3
  5.0 0.3 fusion.4
  5.3 0.1 copy.27
  5.4 0.1 broadcast_in_dim.64
  5.5 0.1 slice.42
  5.6 0.1 copy.28
  5.7 0.1 slice.30
  5.8 0.0 copy-done
  5.8 1.2 %convolution_convert_fusion = bf16[64,768]{1,0:T(8,128)(2,1)S(1)} fusion(bf16[64,768]{1,0:T(8,128)(2,1)} %param.5, bf16[768,768]{1,0:T(8,128)(2,1)S(1)} %copy-done), kind=kOutput, calls=%fused_computation.6 | convolution fusion | flops 75546624 | bytes 1376256 | tf_op jit(solution)/shard_map/dot_general | solution.py:288
  7.0 0.1 reshape.412
  7.2 38.1 %shard_map.55.refs_1_ = bf16[32,400,128]{2,1,0:T(8,128)(2,1)S(1)} custom-call(bf16[400,128]{1,0:T(8,128)(2,1)S(1)} %pad_maximum_fusion.mine_ref), custom_call_target="tpu_custom_call" | custom-call | tf_op jit(solution)/shard_map/pallas_call | solution.py:101
  45.4 0.0 copy-start.1
  45.4 1.7 %copy-done.1 = bf16[32,400,128]{2,1,0:T(8,128)(2,1)} copy-done((bf16[32,400,128]{2,1,0:T(8,128)(2,1)}, bf16[32,400,128]{2,1,0:T(8,128)(2,1)S(1)}, u32[]{:S(2)}) %copy-start.1) | copy-done | bytes 3276824
  47.1 0.2 reshape_reshape.3
  47.4 0.1 reshape_squeeze.7
  47.5 0.1 reshape_squeeze.6
  47.6 0.5 fusion.2
  48.1 0.7 select_reduce_fusion
  48.8 0.2 copy.30.refs_0_
  49.0 0.0 copy-start.2
  49.0 1.9 %copy-done.2 = bf16[32,400,128]{2,1,0:T(8,128)(2,1)S(1)} copy-done((bf16[32,400,128]{2,1,0:T(8,128)(2,1)S(1)}, bf16[32,400,128]{2,1,0:T(8,128)(2,1)}, u32[]{:S(2)}) %copy-start.2) | copy-done | bytes 3276824
  51.0 7.4 %shard_map.56.refs_0_ = bf16[1024,768]{1,0:T(8,128)(2,1)S(1)} custom-call(s32[1024,1]{1,0:T(8,128)S(1)} %copy.30.refs_0_, bf16[32,400,128]{2,1,0:T(8,128)(2,1)S(1)} %copy-done.2), custom_call_target="tpu_custom_call" | custom-call | tf_op jit(solution)/shard_map/pallas_call | solution.py:131
  58.4 0.6 ge.61
  59.0 0.5 mul.93
  59.6 1.0 %copy.32 = s32[1024,1]{1,0:T(8,128)} copy(s32[1024,1]{0,1:T(1,128)S(1)} %bitcast.49) | data formatting | bytes 8192 | tf_op jit(solution)/shard_map/convert_element_type | solution.py:333
  60.6 1.1 %add_select_fusion.refs_2_ = s32[1024,1]{1,0:T(8,128)S(1)} fusion(pred[1024,1]{1,0:T(8,128)(4,1)S(1)} %ge.61, s32[1024,1]{1,0:T(8,128)S(1)} %mul.93, s32[1024,1]{1,0:T(8,128)} %copy.32), kind=kLoop, calls=%fused_computation.14 | loop fusion | flops 2048 | bytes 13312 | tf_op jit(solution)/shard_map/jit(_where)/select_n | solution.py:335
  61.7 11.7 %shard_map.57.refs_0_ = s16[32,80,128]{2,1,0:T(8,128)(2,1)S(1)} custom-call(bf16[1024,768]{1,0:T(8,128)(2,1)S(1)} %shard_map.56.refs_0_, bf16[32,256,768]{2,1,0:T(8,128)(2,1)} %refs_1_.1, s32[1024,1]{1,0:T(8,128)S(1)} %add_select_fusion.refs_2_), custom_call_target="tpu_custom_call" | custom-call | tf_op jit(solution)/shard_map/pallas_call | solution.py:201
  73.4 19.4 %shard_map.58 = s16[32,80,128]{2,1,0:T(8,128)(2,1)S(1)} custom-call(s16[32,80,128]{2,1,0:T(8,128)(2,1)S(1)} %shard_map.57.refs_0_), custom_call_target="tpu_custom_call" | custom-call | tf_op jit(solution)/shard_map/pallas_call | solution.py:262
  92.8 0.2 convert_element_type.85
  93.0 0.1 slice_add_fusion
  93.1 0.8 copy.34
  94.0 0.1 copy.43
  94.1 0.1 div.52
  94.2 0.2 bitcast_multiply_fusion
  94.4 2.2 %gather_fusion.1 = f32[512,256]{1,0:T(8,128)} fusion(f32[1024,256]{1,0:T(8,128)S(1)} %bitcast_multiply_fusion, s32[1024]{0:T(1024)S(1)} %pad_clamp_fusion), kind=kCustom, calls=%fused_computation.1 | custom fusion | bytes 1050624 | tf_op jit(solution)/shard_map/gather | solution.py:350
  (25 shorter events, 0.3 us)
Async XLA Ops:
  0.0 5.8 %copy-start = (bf16[768,768]{1,0:T(8,128)(2,1)S(1)}, bf16[768,768]{1,0:T(8,128)(2,1)}, u32[]{:S(2)}) copy-start(bf16[768,768]{1,0:T(8,128)(2,1)} %param.6) | copy-start | bytes 3538948
  45.4 1.7 %copy-start.1 = (bf16[32,400,128]{2,1,0:T(8,128)(2,1)}, bf16[32,400,128]{2,1,0:T(8,128)(2,1)S(1)}, u32[]{:S(2)}) copy-start(bf16[32,400,128]{2,1,0:T(8,128)(2,1)S(1)} %shard_map.55.refs_1_) | copy-start | bytes 9830404
  49.0 1.9 %copy-start.2 = (bf16[32,400,128]{2,1,0:T(8,128)(2,1)S(1)}, bf16[32,400,128]{2,1,0:T(8,128)(2,1)}, u32[]{:S(2)}) copy-start(bf16[32,400,128]{2,1,0:T(8,128)(2,1)} %copy-done.1) | copy-start | bytes 9830404
